TPU v7x, 32 devices: a whole 2x2x4 slice. The times are simulated.
32 devices in a mesh: grp: 2 (over y), slab: 4 (over z), exp: 2 (over x), sub: 2 (over core).
Axes of the slice: x: 2, y: 2, z: 4, core: 2. Of those that a mesh axis runs over, the one named last changes fastest.
Arguments:
- start_u: float32 [4, 16, 256, 256], P(('grp', 'exp'), 'slab', 'sub'), parts along dimension 0, may hold values from 0.2 to 1
- start_v: float32 [4, 16, 256, 256], P(('grp', 'exp'), 'slab', 'sub'), parts along dimension 0, may hold values from 0 to 0.5
- feed: float32 [32, 256, 256], P(('grp', 'slab'), 'sub'), parts along dimension 0, may hold values from 0.02 to 0.2
- labels: int32 [4, 256, 256], P(('grp', 'exp'), 'sub'), parts along dimension 0, may hold values from 0 to 3
- direction: float32 [32, 256, 256], P(('grp', 'slab'), ('sub', 'exp')), parts along dimension 0, may hold values from -6 to 6
Outputs:
- hess_vec: float32 [32, 256, 256], P(('grp', 'slab'), ('sub', 'exp')), parts along dimension 0
There are 2 independent parts, one for each index of `grp`. A program takes and returns all parts, laid end to end along the dimension named above; each array names one. Nothing has to cross between parts.
All inputs are finite; a program needn't handle non-finite values.
Results may differ from a plain program's by a relative error of at most 0.00002.
Values sent between devices are 32-bit elements; how exact they have to be, the bound alone decides.
A program may use at most 64 MiB of HBM per device.

v0:
```python
import jax
import jax.numpy as jnp
from jax import lax
from jax.sharding import PartitionSpec as P

STEPS = 3


diff_u = 0.15
diff_v = 0.075
kill = 0.06


def extended(cells, sides, width):
    for axis, dim in sides:
        count = lax.axis_size(axis)
        ends = count - 1
        head = lax.slice_in_dim(cells, 0, width, axis=dim)
        tail = lax.slice_in_dim(cells, cells.shape[dim] - width, cells.shape[dim], axis=dim)
        cells = jnp.concatenate(
            [
                lax.ppermute(tail, axis, [(i, (i + 1) % count) for i in range(ends)]),
                cells,
                lax.ppermute(head, axis, [((i + 1) % count, i) for i in range(ends)]),
            ],
            axis=dim,
        )
    return cells


def laplace(padded):
    core = padded[:, :, 1:-1, 1:-1, :]
    total = padded[:, :, 2:, 1:-1, :] + padded[:, :, :-2, 1:-1, :]
    total = total + padded[:, :, 1:-1, 2:, :] + padded[:, :, 1:-1, :-2, :]
    zeros = jnp.zeros_like(core[..., :1])
    total = (
        total
        + jnp.concatenate([core[..., 1:], zeros], -1)
        + jnp.concatenate([zeros, core[..., :-1]], -1)
    )
    return total - 6.0 * core


def state_rims(field):
    return extended(field, (("slab", 2), ("sub", 3)), 1)


def tangent_rims(field):
    return extended(field, (("slab", 2), ("sub", 3)), 1)


def adjoint_rims(field):
    return extended(field, (("slab", 2), ("sub", 3)), 1)


def forward(state, lapped, feed, supply):
    conc_u = state[:, 0]
    conc_v = state[:, 1]
    react = conc_u * conc_v * conc_v
    new_u = conc_u + diff_u * lapped[:, 0] - react + feed * (1.0 - conc_u) + supply
    new_v = conc_v + diff_v * lapped[:, 1] + react - (feed + kill) * conc_v
    return jnp.stack([new_u, new_v], 1)


def tangent(state, lapped, tan, feed, shift):
    conc_u = state[:, 0]
    conc_v = state[:, 1]
    both = conc_u * conc_v
    tan_u = tan[:, 0]
    tan_v = tan[:, 1]
    new_u = (
        tan_u
        + diff_u * lapped[:, 0]
        - (conc_v * conc_v + feed) * tan_u
        - 2.0 * both * tan_v
        + (1.0 - conc_u) * shift
    )
    new_v = (
        tan_v
        + diff_v * lapped[:, 1]
        + conc_v * conc_v * tan_u
        + (2.0 * both - feed - kill) * tan_v
        - conc_v * shift
    )
    return jnp.stack([new_u, new_v], 1)


def first_tangent(state, shift):
    return jnp.stack([(1.0 - state[:, 0]) * shift, -state[:, 1] * shift], 1)


def adjoint(state, lapped, adj, feed):
    conc_u = state[:, 0]
    conc_v = state[:, 1]
    both = conc_u * conc_v
    adj_a = adj[:, 0]
    adj_b = adj[:, 1]
    new_a = (
        adj_a + diff_u * lapped[:, 0] - (conc_v * conc_v + feed) * adj_a + conc_v * conc_v * adj_b
    )
    new_b = adj_b + diff_v * lapped[:, 1] - 2.0 * both * adj_a + (2.0 * both - feed - kill) * adj_b
    return jnp.stack([new_a, new_b], 1)


def per_device(start_u, start_v, feed, labels, direction):
    shift = lax.all_gather(direction, "exp", axis=1, tiled=True)
    supply = (0.1 * labels.astype(jnp.float32))[:, None]
    anchor = jnp.stack([start_u, start_v], 1)
    states = [anchor]
    tan = first_tangent(anchor, shift)
    for step in range(1, STEPS):
        states.append(forward(states[-1], laplace(state_rims(states[-1])), feed, supply))
    for step in range(1, STEPS):
        tan = tangent(states[step], laplace(tangent_rims(tan)), tan, feed, shift)
    adj = tan
    grad = jnp.zeros_like(start_u)
    for step in reversed(range(STEPS)):
        current = states[step]
        grad = grad + (1.0 - current[:, 0]) * adj[:, 0] - current[:, 1] * adj[:, 1]
        if step > 0:
            adj = adjoint(current, laplace(adjoint_rims(adj)), adj, feed)
    partial_sum = jnp.sum(grad, axis=0)
    return lax.psum_scatter(partial_sum, "exp", scatter_dimension=1, tiled=True)


def solution(mesh):
    placed = (
        P(("grp", "exp"), "slab", "sub", None),
        P(("grp", "exp"), "slab", "sub", None),
        P(("grp", "slab"), "sub", None),
        P(("grp", "exp"), "sub", None),
        P(("grp", "slab"), ("sub", "exp"), None),
    )
    return jax.shard_map(
        per_device,
        mesh=mesh,
        in_specs=placed,
        out_specs=P(("grp", "slab"), ("sub", "exp"), None),
        check_vma=False,
    )
```

profile of v0, /device:TPU:0, one launch (start us, length us, event | category | flops | bytes accessed | tf_op | source)
XLA Modules:
  0.0 131.8 jit_solution(13805553212219892593)
XLA Ops:
  6.5 1.2 fusion.128
  7.7 0.0 copy-start
  7.8 5.1 %collective-permute-start.1 = (f32[1,2,1,128,256]{4,3,2,1,0:T(8,128)S(1)}, f32[1,2,1,128,256]{4,3,2,1,0:T(8,128)S(1)}, u32[]{:S(2)}, u32[]{:S(2)}) collective-permute-start(f32[1,2,1,128,256]{4,3,2,1,0:T(8,128)S(1)} %get-tuple-element.43), channel_id=1, source_target_pairs={{0,4},{4,8},{8,12},{1,5},{5,9},{9,13},{2,6},{6,10},{10,14},{3,7},{... | collective-permute-start | bytes 786440 | tf_op jit(solution)/shard_map/ppermute | solution.py:22
  12.8 1.3 collective-permute-start
  14.2 8.4 %all_gather.3 = f32[4,128,256]{2,1,0:T(8,128)S(1)} all-gather(f32[4,64,256]{2,1,0:T(8,128)S(1)} %copy-done.3), channel_id=1, replica_groups=mesh['grp'=2,'slab'=4,'exp'=2,'sub'=2] {'exp'}, dimensions={1}, use_global_device_ids=true | all-gather | bytes 786432 | tf_op jit(solution)/shard_map/all_gather | solution.py:106
  22.6 0.1 fusion.115
  22.7 0.0 copy-start.4
  22.8 4.3 %collective-permute-start.9 = (f32[1,2,1,128,256]{4,3,2,1,0:T(8,128)S(1)}, f32[1,2,1,128,256]{4,3,2,1,0:T(8,128)S(1)}, u32[]{:S(2)}, u32[]{:S(2)}) collective-permute-start(f32[1,2,1,128,256]{4,3,2,1,0:T(8,128)S(1)} %get-tuple-element.47), channel_id=1, source_target_pairs={{0,4},{4,8},{8,12},{1,5},{5,9},{9,13},{2,6},{6,10},{10,14},{3,7},{... | collective-permute-start | bytes 786440 | tf_op jit(solution)/shard_map/ppermute | solution.py:22
  27.1 1.3 collective-permute-start.8
  28.4 0.4 fusion.12
  28.7 0.4 fusion.20
  29.1 2.0 %collective-permute-done.9 = f32[1,2,1,128,256]{4,3,2,1,0:T(8,128)S(1)} collective-permute-done((f32[1,2,1,128,256]{4,3,2,1,0:T(8,128)S(1)}, f32[1,2,1,128,256]{4,3,2,1,0:T(8,128)S(1)}, u32[]{:S(2)}, u32[]{:S(2)}) %collective-permute-start.9) | collective-permute-done | bytes 262176 | tf_op jit(solution)/shard_map/ppermute | solution.py:22
  31.1 4.2 %collective-permute-done.8 = f32[1,2,1,128,256]{4,3,2,1,0:T(8,128)S(1)} collective-permute-done((f32[1,2,1,128,256]{4,3,2,1,0:T(8,128)S(1)}, f32[1,2,1,128,256]{4,3,2,1,0:T(8,128)S(1)}, u32[]{:S(2)}, u32[]{:S(2)}) %collective-permute-start.8) | collective-permute-done | bytes 262176 | tf_op jit(solution)/shard_map/ppermute | solution.py:24
  35.3 1.3 collective-permute-start.10
  36.6 3.0 %collective-permute-start.11 = (f32[1,2,6,1,256]{4,3,2,1,0:T(1,128)S(1)}, f32[1,2,6,1,256]{4,3,2,1,0:T(1,128)S(1)}, u32[]{:S(2)}, u32[]{:S(2)}) collective-permute-start(f32[1,2,6,1,256]{4,3,2,1,0:T(1,128)S(1)} %get-tuple-element.24), channel_id=1, source_target_pairs={{0,1},{2,3},{4,5},{6,7},{8,9},{10,11},{12,13},{14,15},{16,17},{18,... | collective-permute-start | bytes 36872 | tf_op jit(solution)/shard_map/ppermute | solution.py:22
  39.7 0.0 collective-permute-done
  39.7 1.3 collective-permute-start.2
  41.0 3.0 %collective-permute-start.3 = (f32[1,2,6,1,256]{4,3,2,1,0:T(1,128)S(1)}, f32[1,2,6,1,256]{4,3,2,1,0:T(1,128)S(1)}, u32[]{:S(2)}, u32[]{:S(2)}) collective-permute-start(f32[1,2,6,1,256]{4,3,2,1,0:T(1,128)S(1)} %get-tuple-element.22), channel_id=1, source_target_pairs={{0,1},{2,3},{4,5},{6,7},{8,9},{10,11},{12,13},{14,15},{16,17},{18,... | collective-permute-start | bytes 36872 | tf_op jit(solution)/shard_map/ppermute | solution.py:22
  44.1 0.5 fusion.15
  44.6 0.3 collective-permute-done.3
  44.9 0.5 fusion.23
  45.4 0.5 copy-done.2
  45.9 0.5 fusion.98
  46.5 0.3 fusion.93
  46.8 3.5 %collective-permute-start.5 = (f32[1,2,1,128,256]{4,3,2,1,0:T(8,128)S(1)}, f32[1,2,1,128,256]{4,3,2,1,0:T(8,128)S(1)}, u32[]{:S(2)}, u32[]{:S(2)}) collective-permute-start(f32[1,2,1,128,256]{4,3,2,1,0:T(8,128)S(1)} %get-tuple-element.35), channel_id=1, source_target_pairs={{0,4},{4,8},{8,12},{1,5},{5,9},{9,13},{2,6},{6,10},{10,14},{3,7},{... | collective-permute-start | bytes 786440 | tf_op jit(solution)/shard_map/ppermute | solution.py:22
  50.3 1.3 collective-permute-start.4
  51.6 4.6 %collective-permute-start.13 = (f32[1,2,1,128,256]{4,3,2,1,0:T(8,128)S(1)}, f32[1,2,1,128,256]{4,3,2,1,0:T(8,128)S(1)}, u32[]{:S(2)}, u32[]{:S(2)}) collective-permute-start(f32[1,2,1,128,256]{4,3,2,1,0:T(8,128)S(1)} %get-tuple-element.39), channel_id=1, source_target_pairs={{0,4},{4,8},{8,12},{1,5},{5,9},{9,13},{2,6},{6,10},{10,14},{3,7},{... | collective-permute-start | bytes 786440 | tf_op jit(solution)/shard_map/ppermute | solution.py:22
  56.2 1.3 collective-permute-start.12
  57.5 0.4 fusion.16
  57.9 0.4 fusion.8
  58.2 2.4 %collective-permute-done.4 = f32[1,2,1,128,256]{4,3,2,1,0:T(8,128)S(1)} collective-permute-done((f32[1,2,1,128,256]{4,3,2,1,0:T(8,128)S(1)}, f32[1,2,1,128,256]{4,3,2,1,0:T(8,128)S(1)}, u32[]{:S(2)}, u32[]{:S(2)}) %collective-permute-start.4) | collective-permute-done | bytes 262176 | tf_op jit(solution)/shard_map/ppermute | solution.py:24
  60.7 1.3 collective-permute-start.6
  62.0 3.0 %collective-permute-start.7 = (f32[1,2,6,1,256]{4,3,2,1,0:T(1,128)S(1)}, f32[1,2,6,1,256]{4,3,2,1,0:T(1,128)S(1)}, u32[]{:S(2)}, u32[]{:S(2)}) collective-permute-start(f32[1,2,6,1,256]{4,3,2,1,0:T(1,128)S(1)} %get-tuple-element.18), channel_id=1, source_target_pairs={{0,1},{2,3},{4,5},{6,7},{8,9},{10,11},{12,13},{14,15},{16,17},{18,... | collective-permute-start | bytes 36872 | tf_op jit(solution)/shard_map/ppermute | solution.py:22
  65.0 0.0 collective-permute-done.13
  65.0 1.1 collective-permute-done.12
  66.1 1.3 collective-permute-start.14
  67.4 3.0 %collective-permute-start.15 = (f32[1,2,6,1,256]{4,3,2,1,0:T(1,128)S(1)}, f32[1,2,6,1,256]{4,3,2,1,0:T(1,128)S(1)}, u32[]{:S(2)}, u32[]{:S(2)}) collective-permute-start(f32[1,2,6,1,256]{4,3,2,1,0:T(1,128)S(1)} %get-tuple-element.20), channel_id=1, source_target_pairs={{0,1},{2,3},{4,5},{6,7},{8,9},{10,11},{12,13},{14,15},{16,17},{18,... | collective-permute-start | bytes 36872 | tf_op jit(solution)/shard_map/ppermute | solution.py:22
  70.5 0.5 fusion.19
  71.0 0.3 collective-permute-done.15
  71.2 0.5 fusion.11
  71.8 0.5 fusion.88
  72.3 0.3 fusion.79
  72.6 3.5 %collective-permute-start.17 = (f32[1,2,1,128,256]{4,3,2,1,0:T(8,128)S(1)}, f32[1,2,1,128,256]{4,3,2,1,0:T(8,128)S(1)}, u32[]{:S(2)}, u32[]{:S(2)}) collective-permute-start(f32[1,2,1,128,256]{4,3,2,1,0:T(8,128)S(1)} %get-tuple-element.31), channel_id=1, source_target_pairs={{0,4},{4,8},{8,12},{1,5},{5,9},{9,13},{2,6},{6,10},{10,14},{3,7},{... | collective-permute-start | bytes 786440 | tf_op jit(solution)/shard_map/ppermute | solution.py:22
  76.1 1.3 collective-permute-start.16
  77.4 4.7 %collective-permute-done.17 = f32[1,2,1,128,256]{4,3,2,1,0:T(8,128)S(1)} collective-permute-done((f32[1,2,1,128,256]{4,3,2,1,0:T(8,128)S(1)}, f32[1,2,1,128,256]{4,3,2,1,0:T(8,128)S(1)}, u32[]{:S(2)}, u32[]{:S(2)}) %collective-permute-start.17) | collective-permute-done | bytes 262176 | tf_op jit(solution)/shard_map/ppermute | solution.py:22
  82.1 4.1 %collective-permute-done.16 = f32[1,2,1,128,256]{4,3,2,1,0:T(8,128)S(1)} collective-permute-done((f32[1,2,1,128,256]{4,3,2,1,0:T(8,128)S(1)}, f32[1,2,1,128,256]{4,3,2,1,0:T(8,128)S(1)}, u32[]{:S(2)}, u32[]{:S(2)}) %collective-permute-start.16) | collective-permute-done | bytes 262176 | tf_op jit(solution)/shard_map/ppermute | solution.py:24
  86.3 1.3 collective-permute-start.18
  87.6 3.0 %collective-permute-start.19 = (f32[1,2,6,1,256]{4,3,2,1,0:T(1,128)S(1)}, f32[1,2,6,1,256]{4,3,2,1,0:T(1,128)S(1)}, u32[]{:S(2)}, u32[]{:S(2)}) collective-permute-start(f32[1,2,6,1,256]{4,3,2,1,0:T(1,128)S(1)} %get-tuple-element.16), channel_id=1, source_target_pairs={{0,1},{2,3},{4,5},{6,7},{8,9},{10,11},{12,13},{14,15},{16,17},{18,... | collective-permute-start | bytes 36872 | tf_op jit(solution)/shard_map/ppermute | solution.py:22
  90.6 0.4 fusion.4
  91.0 0.4 collective-permute-done.19
  91.4 0.5 fusion.7
  91.9 0.3 fusion.130
  92.3 2.2 %collective-permute-start.21 = (f32[1,2,1,128,256]{4,3,2,1,0:T(8,128)S(1)}, f32[1,2,1,128,256]{4,3,2,1,0:T(8,128)S(1)}, u32[]{:S(2)}, u32[]{:S(2)}) collective-permute-start(f32[1,2,1,128,256]{4,3,2,1,0:T(8,128)S(1)} %get-tuple-element.27), channel_id=1, source_target_pairs={{0,4},{4,8},{8,12},{1,5},{5,9},{9,13},{2,6},{6,10},{10,14},{3,7},{... | collective-permute-start | bytes 786440 | tf_op jit(solution)/shard_map/ppermute | solution.py:22
  94.5 1.3 collective-permute-start.20
  95.8 4.7 %collective-permute-done.21 = f32[1,2,1,128,256]{4,3,2,1,0:T(8,128)S(1)} collective-permute-done((f32[1,2,1,128,256]{4,3,2,1,0:T(8,128)S(1)}, f32[1,2,1,128,256]{4,3,2,1,0:T(8,128)S(1)}, u32[]{:S(2)}, u32[]{:S(2)}) %collective-permute-start.21) | collective-permute-done | bytes 262176 | tf_op jit(solution)/shard_map/ppermute | solution.py:22
  100.5 4.1 %collective-permute-done.20 = f32[1,2,1,128,256]{4,3,2,1,0:T(8,128)S(1)} collective-permute-done((f32[1,2,1,128,256]{4,3,2,1,0:T(8,128)S(1)}, f32[1,2,1,128,256]{4,3,2,1,0:T(8,128)S(1)}, u32[]{:S(2)}, u32[]{:S(2)}) %collective-permute-start.20) | collective-permute-done | bytes 262176 | tf_op jit(solution)/shard_map/ppermute | solution.py:24
  104.7 1.3 collective-permute-start.22
  106.0 3.0 %collective-permute-start.23 = (f32[1,2,6,1,256]{4,3,2,1,0:T(1,128)S(1)}, f32[1,2,6,1,256]{4,3,2,1,0:T(1,128)S(1)}, u32[]{:S(2)}, u32[]{:S(2)}) collective-permute-start(f32[1,2,6,1,256]{4,3,2,1,0:T(1,128)S(1)} %get-tuple-element.14), channel_id=1, source_target_pairs={{0,1},{2,3},{4,5},{6,7},{8,9},{10,11},{12,13},{14,15},{16,17},{18,... | collective-permute-start | bytes 36872 | tf_op jit(solution)/shard_map/ppermute | solution.py:22
  109.0 0.4 fusion
  109.4 0.4 collective-permute-done.23
  109.8 0.5 fusion.3
  110.3 1.7 %fusion.60 = f32[4,128,256]{2,1,0:T(8,128)} fusion(f32[1,4,128,256]{3,2,1,0:T(8,128)S(1)} %copy-done, f32[1,2,4,128,256]{4,3,2,1,0:T(8,128)S(1)} %fusion.3, f32[1,4,128,256]{3,2,1,0:T(8,128)S(1)} %get-tuple-element.10, f32[1,4,128,256]{3,2,1,0:T(8,128)S(1)} %get-tuple-element.7, f32[1,4,128,256]{3,2,1,0:T(8,128)S(1)} %fusion.79, ...), kind=kLoop, calls=%fused_computation.188 | loop fusion | flops 6553600 | bytes 7340032 | tf_op jit(solution)/shard_map/reduce_sum | solution.py:122
  112.0 0.0 reduce-scatter.2.cloned.1.call-update
  112.0 12.9 %reduce-scatter.2.cloned.1.call-done = f32[4,64,256]{2,1,0:T(8,128)} async-done(((f32[4,128,256]{2,1,0:T(8,128)}), f32[4,64,256]{2,1,0:T(8,128)}) %reduce-scatter.2.cloned.1.call-update) | async-done | bytes 262160 | tf_op jit(solution)/shard_map/reduce_scatter | solution.py:123
  (30 shorter events, 0.4 us)
Async XLA Ops:
  6.5 118.4 %reduce-scatter.2.cloned.1.call-start = ((), (), s32[]{:S(2)}) async-start(), calls=%async_computation.1 | async-start | bytes 786432 | tf_op jit(solution)/shard_map/reduce_scatter | solution.py:123
  6.5 7.6 %copy-start.3 = (f32[4,64,256]{2,1,0:T(8,128)S(1)}, f32[4,64,256]{2,1,0:T(8,128)}, u32[]{:S(2)}) copy-start(f32[4,64,256]{2,1,0:T(8,128)} %param.9) | copy-start | bytes 786436
  6.5 16.1 %copy-start.1 = (f32[1,4,128,256]{3,2,1,0:T(8,128)S(1)}, f32[1,4,128,256]{3,2,1,0:T(8,128)}, u32[]{:S(2)}) copy-start(f32[1,4,128,256]{3,2,1,0:T(8,128)} %param.5) | copy-start | bytes 1572868
  7.7 14.9 %copy-start = (f32[1,4,128,256]{3,2,1,0:T(8,128)S(1)}, f32[1,4,128,256]{3,2,1,0:T(8,128)}, u32[]{:S(2)}) copy-start(f32[1,4,128,256]{3,2,1,0:T(8,128)} %param.6) | copy-start | bytes 1572868
  7.8 31.9 %collective-permute-start.1 = (f32[1,2,1,128,256]{4,3,2,1,0:T(8,128)S(1)}, f32[1,2,1,128,256]{4,3,2,1,0:T(8,128)S(1)}, u32[]{:S(2)}, u32[]{:S(2)}) collective-permute-start(f32[1,2,1,128,256]{4,3,2,1,0:T(8,128)S(1)} %get-tuple-element.43), channel_id=1, source_target_pairs={{0,4},{4,8},{8,12},{1,5},{5,9},{9,13},{2,6},{6,10},{10,14},{3,7},{... | collective-permute-start | bytes 786440 | tf_op jit(solution)/shard_map/ppermute | solution.py:22
  12.8 26.9 %collective-permute-start = (f32[1,2,1,128,256]{4,3,2,1,0:T(8,128)S(1)}, f32[1,2,1,128,256]{4,3,2,1,0:T(8,128)S(1)}, u32[]{:S(2)}, u32[]{:S(2)}) collective-permute-start(f32[1,2,1,128,256]{4,3,2,1,0:T(8,128)S(1)} %get-tuple-element.44), channel_id=1, source_target_pairs={{4,0},{8,4},{12,8},{5,1},{9,5},{13,9},{6,2},{10,6},{14,10},{7,3},{... | collective-permute-start | bytes 786440 | tf_op jit(solution)/shard_map/ppermute | solution.py:24
  22.7 5.6 %copy-start.4 = (s32[1,128,256]{2,1,0:T(8,128)S(1)}, s32[1,128,256]{2,1,0:T(8,128)}, u32[]{:S(2)}) copy-start(s32[1,128,256]{2,1,0:T(8,128)} %param.8) | copy-start | bytes 393220
  22.8 8.3 %collective-permute-start.9 = (f32[1,2,1,128,256]{4,3,2,1,0:T(8,128)S(1)}, f32[1,2,1,128,256]{4,3,2,1,0:T(8,128)S(1)}, u32[]{:S(2)}, u32[]{:S(2)}) collective-permute-start(f32[1,2,1,128,256]{4,3,2,1,0:T(8,128)S(1)} %get-tuple-element.47), channel_id=1, source_target_pairs={{0,4},{4,8},{8,12},{1,5},{5,9},{9,13},{2,6},{6,10},{10,14},{3,7},{... | collective-permute-start | bytes 786440 | tf_op jit(solution)/shard_map/ppermute | solution.py:22
  27.1 8.3 %collective-permute-start.8 = (f32[1,2,1,128,256]{4,3,2,1,0:T(8,128)S(1)}, f32[1,2,1,128,256]{4,3,2,1,0:T(8,128)S(1)}, u32[]{:S(2)}, u32[]{:S(2)}) collective-permute-start(f32[1,2,1,128,256]{4,3,2,1,0:T(8,128)S(1)} %get-tuple-element.48), channel_id=1, source_target_pairs={{4,0},{8,4},{12,8},{5,1},{9,5},{13,9},{6,2},{10,6},{14,10},{7,3},{... | collective-permute-start | bytes 786440 | tf_op jit(solution)/shard_map/ppermute | solution.py:24
  35.3 8.7 %collective-permute-start.10 = (f32[1,2,6,1,256]{4,3,2,1,0:T(1,128)S(1)}, f32[1,2,6,1,256]{4,3,2,1,0:T(1,128)S(1)}, u32[]{:S(2)}, u32[]{:S(2)}) collective-permute-start(f32[1,2,6,1,256]{4,3,2,1,0:T(1,128)S(1)} %get-tuple-element.23), channel_id=1, source_target_pairs={{1,0},{3,2},{5,4},{7,6},{9,8},{11,10},{13,12},{15,14},{17,16},{19,... | collective-permute-start | bytes 36872 | tf_op jit(solution)/shard_map/ppermute | solution.py:24
  36.6 7.4 %collective-permute-start.11 = (f32[1,2,6,1,256]{4,3,2,1,0:T(1,128)S(1)}, f32[1,2,6,1,256]{4,3,2,1,0:T(1,128)S(1)}, u32[]{:S(2)}, u32[]{:S(2)}) collective-permute-start(f32[1,2,6,1,256]{4,3,2,1,0:T(1,128)S(1)} %get-tuple-element.24), channel_id=1, source_target_pairs={{0,1},{2,3},{4,5},{6,7},{8,9},{10,11},{12,13},{14,15},{16,17},{18,... | collective-permute-start | bytes 36872 | tf_op jit(solution)/shard_map/ppermute | solution.py:22
  39.7 4.9 %collective-permute-start.2 = (f32[1,2,6,1,256]{4,3,2,1,0:T(1,128)S(1)}, f32[1,2,6,1,256]{4,3,2,1,0:T(1,128)S(1)}, u32[]{:S(2)}, u32[]{:S(2)}) collective-permute-start(f32[1,2,6,1,256]{4,3,2,1,0:T(1,128)S(1)} %get-tuple-element.21), channel_id=1, source_target_pairs={{1,0},{3,2},{5,4},{7,6},{9,8},{11,10},{13,12},{15,14},{17,16},{19,... | collective-permute-start | bytes 36872 | tf_op jit(solution)/shard_map/ppermute | solution.py:24
  41.0 3.9 %collective-permute-start.3 = (f32[1,2,6,1,256]{4,3,2,1,0:T(1,128)S(1)}, f32[1,2,6,1,256]{4,3,2,1,0:T(1,128)S(1)}, u32[]{:S(2)}, u32[]{:S(2)}) collective-permute-start(f32[1,2,6,1,256]{4,3,2,1,0:T(1,128)S(1)} %get-tuple-element.22), channel_id=1, source_target_pairs={{0,1},{2,3},{4,5},{6,7},{8,9},{10,11},{12,13},{14,15},{16,17},{18,... | collective-permute-start | bytes 36872 | tf_op jit(solution)/shard_map/ppermute | solution.py:22
  44.9 1.0 copy-start.2
  46.8 11.4 %collective-permute-start.5 = (f32[1,2,1,128,256]{4,3,2,1,0:T(8,128)S(1)}, f32[1,2,1,128,256]{4,3,2,1,0:T(8,128)S(1)}, u32[]{:S(2)}, u32[]{:S(2)}) collective-permute-start(f32[1,2,1,128,256]{4,3,2,1,0:T(8,128)S(1)} %get-tuple-element.35), channel_id=1, source_target_pairs={{0,4},{4,8},{8,12},{1,5},{5,9},{9,13},{2,6},{6,10},{10,14},{3,7},{... | collective-permute-start | bytes 786440 | tf_op jit(solution)/shard_map/ppermute | solution.py:22
  50.3 10.4 %collective-permute-start.4 = (f32[1,2,1,128,256]{4,3,2,1,0:T(8,128)S(1)}, f32[1,2,1,128,256]{4,3,2,1,0:T(8,128)S(1)}, u32[]{:S(2)}, u32[]{:S(2)}) collective-permute-start(f32[1,2,1,128,256]{4,3,2,1,0:T(8,128)S(1)} %get-tuple-element.36), channel_id=1, source_target_pairs={{4,0},{8,4},{12,8},{5,1},{9,5},{13,9},{6,2},{10,6},{14,10},{7,3},{... | collective-permute-start | bytes 786440 | tf_op jit(solution)/shard_map/ppermute | solution.py:24
  51.6 13.4 %collective-permute-start.13 = (f32[1,2,1,128,256]{4,3,2,1,0:T(8,128)S(1)}, f32[1,2,1,128,256]{4,3,2,1,0:T(8,128)S(1)}, u32[]{:S(2)}, u32[]{:S(2)}) collective-permute-start(f32[1,2,1,128,256]{4,3,2,1,0:T(8,128)S(1)} %get-tuple-element.39), channel_id=1, source_target_pairs={{0,4},{4,8},{8,12},{1,5},{5,9},{9,13},{2,6},{6,10},{10,14},{3,7},{... | collective-permute-start | bytes 786440 | tf_op jit(solution)/shard_map/ppermute | solution.py:22
  56.2 9.9 %collective-permute-start.12 = (f32[1,2,1,128,256]{4,3,2,1,0:T(8,128)S(1)}, f32[1,2,1,128,256]{4,3,2,1,0:T(8,128)S(1)}, u32[]{:S(2)}, u32[]{:S(2)}) collective-permute-start(f32[1,2,1,128,256]{4,3,2,1,0:T(8,128)S(1)} %get-tuple-element.40), channel_id=1, source_target_pairs={{4,0},{8,4},{12,8},{5,1},{9,5},{13,9},{6,2},{10,6},{14,10},{7,3},{... | collective-permute-start | bytes 786440 | tf_op jit(solution)/shard_map/ppermute | solution.py:24
  60.7 9.8 %collective-permute-start.6 = (f32[1,2,6,1,256]{4,3,2,1,0:T(1,128)S(1)}, f32[1,2,6,1,256]{4,3,2,1,0:T(1,128)S(1)}, u32[]{:S(2)}, u32[]{:S(2)}) collective-permute-start(f32[1,2,6,1,256]{4,3,2,1,0:T(1,128)S(1)} %get-tuple-element.17), channel_id=1, source_target_pairs={{1,0},{3,2},{5,4},{7,6},{9,8},{11,10},{13,12},{15,14},{17,16},{19,... | collective-permute-start | bytes 36872 | tf_op jit(solution)/shard_map/ppermute | solution.py:24
  62.0 8.5 %collective-permute-start.7 = (f32[1,2,6,1,256]{4,3,2,1,0:T(1,128)S(1)}, f32[1,2,6,1,256]{4,3,2,1,0:T(1,128)S(1)}, u32[]{:S(2)}, u32[]{:S(2)}) collective-permute-start(f32[1,2,6,1,256]{4,3,2,1,0:T(1,128)S(1)} %get-tuple-element.18), channel_id=1, source_target_pairs={{0,1},{2,3},{4,5},{6,7},{8,9},{10,11},{12,13},{14,15},{16,17},{18,... | collective-permute-start | bytes 36872 | tf_op jit(solution)/shard_map/ppermute | solution.py:22
  66.1 4.9 %collective-permute-start.14 = (f32[1,2,6,1,256]{4,3,2,1,0:T(1,128)S(1)}, f32[1,2,6,1,256]{4,3,2,1,0:T(1,128)S(1)}, u32[]{:S(2)}, u32[]{:S(2)}) collective-permute-start(f32[1,2,6,1,256]{4,3,2,1,0:T(1,128)S(1)} %get-tuple-element.19), channel_id=1, source_target_pairs={{1,0},{3,2},{5,4},{7,6},{9,8},{11,10},{13,12},{15,14},{17,16},{19,... | collective-permute-start | bytes 36872 | tf_op jit(solution)/shard_map/ppermute | solution.py:24
  67.4 3.9 %collective-permute-start.15 = (f32[1,2,6,1,256]{4,3,2,1,0:T(1,128)S(1)}, f32[1,2,6,1,256]{4,3,2,1,0:T(1,128)S(1)}, u32[]{:S(2)}, u32[]{:S(2)}) collective-permute-start(f32[1,2,6,1,256]{4,3,2,1,0:T(1,128)S(1)} %get-tuple-element.20), channel_id=1, source_target_pairs={{0,1},{2,3},{4,5},{6,7},{8,9},{10,11},{12,13},{14,15},{16,17},{18,... | collective-permute-start | bytes 36872 | tf_op jit(solution)/shard_map/ppermute | solution.py:22
  72.6 9.5 %collective-permute-start.17 = (f32[1,2,1,128,256]{4,3,2,1,0:T(8,128)S(1)}, f32[1,2,1,128,256]{4,3,2,1,0:T(8,128)S(1)}, u32[]{:S(2)}, u32[]{:S(2)}) collective-permute-start(f32[1,2,1,128,256]{4,3,2,1,0:T(8,128)S(1)} %get-tuple-element.31), channel_id=1, source_target_pairs={{0,4},{4,8},{8,12},{1,5},{5,9},{9,13},{2,6},{6,10},{10,14},{3,7},{... | collective-permute-start | bytes 786440 | tf_op jit(solution)/shard_map/ppermute | solution.py:22
  76.1 10.2 %collective-permute-start.16 = (f32[1,2,1,128,256]{4,3,2,1,0:T(8,128)S(1)}, f32[1,2,1,128,256]{4,3,2,1,0:T(8,128)S(1)}, u32[]{:S(2)}, u32[]{:S(2)}) collective-permute-start(f32[1,2,1,128,256]{4,3,2,1,0:T(8,128)S(1)} %get-tuple-element.32), channel_id=1, source_target_pairs={{4,0},{8,4},{12,8},{5,1},{9,5},{13,9},{6,2},{10,6},{14,10},{7,3},{... | collective-permute-start | bytes 786440 | tf_op jit(solution)/shard_map/ppermute | solution.py:24
  86.3 4.7 %collective-permute-start.18 = (f32[1,2,6,1,256]{4,3,2,1,0:T(1,128)S(1)}, f32[1,2,6,1,256]{4,3,2,1,0:T(1,128)S(1)}, u32[]{:S(2)}, u32[]{:S(2)}) collective-permute-start(f32[1,2,6,1,256]{4,3,2,1,0:T(1,128)S(1)} %get-tuple-element.15), channel_id=1, source_target_pairs={{1,0},{3,2},{5,4},{7,6},{9,8},{11,10},{13,12},{15,14},{17,16},{19,... | collective-permute-start | bytes 36872 | tf_op jit(solution)/shard_map/ppermute | solution.py:24
  87.6 3.9 %collective-permute-start.19 = (f32[1,2,6,1,256]{4,3,2,1,0:T(1,128)S(1)}, f32[1,2,6,1,256]{4,3,2,1,0:T(1,128)S(1)}, u32[]{:S(2)}, u32[]{:S(2)}) collective-permute-start(f32[1,2,6,1,256]{4,3,2,1,0:T(1,128)S(1)} %get-tuple-element.16), channel_id=1, source_target_pairs={{0,1},{2,3},{4,5},{6,7},{8,9},{10,11},{12,13},{14,15},{16,17},{18,... | collective-permute-start | bytes 36872 | tf_op jit(solution)/shard_map/ppermute | solution.py:22
  92.3 8.2 %collective-permute-start.21 = (f32[1,2,1,128,256]{4,3,2,1,0:T(8,128)S(1)}, f32[1,2,1,128,256]{4,3,2,1,0:T(8,128)S(1)}, u32[]{:S(2)}, u32[]{:S(2)}) collective-permute-start(f32[1,2,1,128,256]{4,3,2,1,0:T(8,128)S(1)} %get-tuple-element.27), channel_id=1, source_target_pairs={{0,4},{4,8},{8,12},{1,5},{5,9},{9,13},{2,6},{6,10},{10,14},{3,7},{... | collective-permute-start | bytes 786440 | tf_op jit(solution)/shard_map/ppermute | solution.py:22
  94.5 10.2 %collective-permute-start.20 = (f32[1,2,1,128,256]{4,3,2,1,0:T(8,128)S(1)}, f32[1,2,1,128,256]{4,3,2,1,0:T(8,128)S(1)}, u32[]{:S(2)}, u32[]{:S(2)}) collective-permute-start(f32[1,2,1,128,256]{4,3,2,1,0:T(8,128)S(1)} %get-tuple-element.28), channel_id=1, source_target_pairs={{4,0},{8,4},{12,8},{5,1},{9,5},{13,9},{6,2},{10,6},{14,10},{7,3},{... | collective-permute-start | bytes 786440 | tf_op jit(solution)/shard_map/ppermute | solution.py:24
  104.7 4.7 %collective-permute-start.22 = (f32[1,2,6,1,256]{4,3,2,1,0:T(1,128)S(1)}, f32[1,2,6,1,256]{4,3,2,1,0:T(1,128)S(1)}, u32[]{:S(2)}, u32[]{:S(2)}) collective-permute-start(f32[1,2,6,1,256]{4,3,2,1,0:T(1,128)S(1)} %get-tuple-element.13), channel_id=1, source_target_pairs={{1,0},{3,2},{5,4},{7,6},{9,8},{11,10},{13,12},{15,14},{17,16},{19,... | collective-permute-start | bytes 36872 | tf_op jit(solution)/shard_map/ppermute | solution.py:24
  106.0 3.9 %collective-permute-start.23 = (f32[1,2,6,1,256]{4,3,2,1,0:T(1,128)S(1)}, f32[1,2,6,1,256]{4,3,2,1,0:T(1,128)S(1)}, u32[]{:S(2)}, u32[]{:S(2)}) collective-permute-start(f32[1,2,6,1,256]{4,3,2,1,0:T(1,128)S(1)} %get-tuple-element.14), channel_id=1, source_target_pairs={{0,1},{2,3},{4,5},{6,7},{8,9},{10,11},{12,13},{14,15},{16,17},{18,... | collective-permute-start | bytes 36872 | tf_op jit(solution)/shard_map/ppermute | solution.py:22
Sparse Core Ops, SparseCore 0:
  112.1 12.7 reduce-scatter.1
where the time goes:
time: 133 us; the launch traced here: 132 us
  starting transfers between devices  56.8 us (43%)
  waiting for transfers between devices  41.9 us (32%)
  between operations  13.8 us (10%)
  other arithmetic  10.4 us (8%)
  blocking collectives  8.44 us (6%)
    ppermute x12, starting transfers between devices, extended(): lax.ppermute(tail, axis, [(i, (i + 1) % count) for i in range(ends)])  41.3 us
    ppermute x12, waiting for transfers between devices, extended(): lax.ppermute(head, axis, [((i + 1) % count, i) for i in range(ends)])  16 us
    ppermute x12, starting transfers between devices, extended(): lax.ppermute(head, axis, [((i + 1) % count, i) for i in range(ends)])  15.5 us
    reduce_scatter x1, waiting for transfers between devices, per_device(): return lax.psum_scatter(partial_sum, 'exp', scatter_dimension=1, tiled=True)  12.9 us
    ppermute x12, waiting for transfers between devices, extended(): lax.ppermute(tail, axis, [(i, (i + 1) % count) for i in range(ends)])  12.9 us
    all_gather x1, blocking collectives, per_device(): shift = lax.all_gather(direction, 'exp', axis=1, tiled=True)  8.44 us
    sub x6, other arithmetic, laplace(): return total - 6.0 * core  3.06 us
  transfers between devices with their start and end apart: 25, of which 13 were waited for; matrix products, arithmetic and copies ran while one was open for 3% of the time, Pallas kernels for 0%

commit v1 on v0

v1 whole, which is shorter than its diff:
```python
import functools

import jax
import jax.numpy as jnp
from jax import lax
from jax.experimental import pallas as pl
from jax.experimental.pallas import tpu as pltpu
from jax.sharding import PartitionSpec as P

diff_u = 0.15
diff_v = 0.075
kill = 0.06

EDGE = 8
PAD = 8
CHUNK = 32
LO, HI = 2, 5
MESH = pl.DeviceIdType.MESH


def kernel(
    slabs, exps,
    u_in, v_in, feed_in, lab_in, dir_in, out,
    U0, V0, D, F, LAB, U1, V1, U2, V2, P1, Q1, P2, Q2, A3, B3, A2, B2,
    C, CN, G, R, send, recv, local,
):
    own, width = u_in.shape[1], u_in.shape[2]
    rows = own + EDGE
    part = own // exps
    grp, slab = lax.axis_index("grp"), lax.axis_index("slab")
    exp, sub = lax.axis_index("exp"), lax.axis_index("sub")
    has = (slab > 0, slab < slabs - 1)
    mate = 1 - sub

    def row(value):
        return pl.multiple_of(value, 8)

    start = row(PAD + EDGE * sub)
    edge_in = row((own - EDGE) * (1 - sub))
    edge_out = row(PAD + own * sub)
    mine = row(start + part * exp)

    def peer(side=None, step=0, other=False):
        z = slab if side is None else slab + (2 * side - 1)
        return (grp, z, lax.rem(exp + step, exps), mate if other else sub)

    count = [0]
    pending = []

    def remote(src, dst, target, sends=None, gets=None):
        i = count[0]
        count[0] += 1
        copy = pltpu.make_async_remote_copy(
            src_ref=src, dst_ref=dst, send_sem=send.at[i], recv_sem=recv.at[i],
            device_id=target, device_id_type=MESH,
        )
        if sends is None:
            copy.start()
        else:
            pl.when(sends)(copy.start)
        pending.append((sends, copy))

        def arrived():
            if gets is None:
                copy.wait_recv()
            else:
                pl.when(gets)(copy.wait_recv)

        return arrived

    loads = []
    for i, (src, dst) in enumerate([
        (u_in, U0.at[LO : HI + 1, pl.ds(start, own)]),
        (v_in, V0.at[LO : HI + 1, pl.ds(start, own)]),
        (feed_in, F.at[LO : HI + 1, pl.ds(start, own)]),
        (lab_in, LAB.at[pl.ds(start, own)]),
        (dir_in, D.at[LO : HI + 1, pl.ds(mine, part)]),
    ]):
        copy = pltpu.make_async_copy(src, dst, local.at[i])
        copy.start()
        loads.append(copy)

    barrier = pltpu.get_barrier_semaphore()

    def greet(target):
        pl.semaphore_signal(barrier, inc=1, device_id=target, device_id_type=MESH)

    greet(peer(other=True))
    for step in range(1, exps):
        greet(peer(step=step))
    for side in (0, 1):
        @pl.when(has[side])
        def _():
            greet(peer(side))
            greet(peer(side, other=True))

    for ref in (U0, V0, U1, V1, P1, Q1, P2, Q2, A3, B3, A2, B2):
        blank = jnp.zeros((ref.shape[0], PAD, width), jnp.float32)
        ref[:, :PAD, :] = blank
        ref[:, PAD + rows :, :] = blank
    for ref in (A2, B2):
        for p in (LO - 1, HI + 1):
            ref[p] = jnp.zeros(ref.shape[1:], jnp.float32)
    for side in (0, 1):
        @pl.when(jnp.logical_not(has[side]))
        def _():
            for ref in (U0, V0, D):
                for p in ((0, 1), (6, 7))[side]:
                    ref[p] = jnp.zeros(ref.shape[1:], jnp.float32)
            for ref in (F, A3, B3):
                ref[(1, 6)[side]] = jnp.zeros(ref.shape[1:], jnp.float32)
            CN[side] = jnp.zeros(CN.shape[1:], jnp.float32)

    near = jnp.where(has[0], 1, 0) + jnp.where(has[1], 1, 0)
    pl.semaphore_wait(barrier, exps + 2 * near)

    outer = (0, 3)
    second = (1, 2)
    first_in = (6, 1)
    second_in = (7, 0)
    pair = ((0, 2), (2, 4))
    pair_in = ((6, 8), (0, 2))

    got_dir, got_feed, got_one, got_two = [], [], [], []
    for side in (0, 1):
        a, b = pair[side]
        c, d = pair_in[side]
        got_dir.append(remote(
            dir_in.at[a:b], D.at[c:d, pl.ds(mine, part)], peer(side), has[side], has[1 - side]))
        got_feed.append(remote(
            feed_in.at[outer[side], pl.ds(row(part * exp), part)],
            F.at[first_in[side], pl.ds(mine, part)], peer(side), has[side], has[1 - side]))
    got_mate = []
    for src, dst in ((u_in, U0), (v_in, V0), (feed_in, F)):
        got_mate.append(remote(
            src.at[:, pl.ds(edge_in, EDGE)], dst.at[LO : HI + 1, pl.ds(edge_out, EDGE)],
            peer(other=True)))
    got_mate.append(remote(
        lab_in.at[pl.ds(edge_in, EDGE)], LAB.at[pl.ds(edge_out, EDGE)], peer(other=True)))
    got_rows = [
        remote(dir_in, D.at[LO : HI + 1, pl.ds(mine, part)], peer(step=step))
        for step in range(1, exps)
    ]
    for side in (0, 1):
        for src, dst in ((u_in, U0), (v_in, V0)):
            got_one.append(remote(
                src.at[outer[side]], dst.at[first_in[side], pl.ds(start, own)],
                peer(side), has[side], has[1 - side]))
    for side in (0, 1):
        a, b = pair[side]
        c, d = pair_in[side]
        for src, dst in ((u_in, U0), (v_in, V0)):
            got_one.append(remote(
                src.at[a:b, pl.ds(edge_in, EDGE)], dst.at[c:d, pl.ds(edge_out, EDGE)],
                peer(side, other=True), has[side], has[1 - side]))
    for side in (0, 1):
        for src, dst in ((u_in, U0), (v_in, V0)):
            got_two.append(remote(
                src.at[second[side]], dst.at[second_in[side], pl.ds(start, own)],
                peer(side), has[side], has[1 - side]))

    def sweep(planes, body, first=PAD, length=rows):
        begin, stride, number = planes

        def plane(i, carry):
            p = begin + stride * i

            def block(j, inner):
                body(p, row(first + j * CHUNK), CHUNK)
                return inner

            lax.fori_loop(0, length // CHUNK, block, 0)
            if length % CHUNK:
                body(p, row(first + length // CHUNK * CHUNK), length % CHUNK)
            return carry

        lax.fori_loop(0, number, plane, 0)

    def held(ref, p, r, n):
        return ref[p, pl.ds(r, n), :]

    def lap(ref, p, r, n):
        core = held(ref, p, r, n)
        wide = ref[p, pl.ds(row(r - 8), n + 16), :]
        lane = lax.broadcasted_iota(jnp.int32, core.shape, 1)
        total = held(ref, p + 1, r, n) + held(ref, p - 1, r, n)
        total = total + wide[9 : 9 + n] + wide[7 : 7 + n]
        total = total + jnp.where(lane == width - 1, 0.0, pltpu.roll(core, width - 1, 1))
        total = total + jnp.where(lane == 0, 0.0, pltpu.roll(core, 1, 1))
        return core, total - 6.0 * core

    def halo_mask(p):
        there = jnp.where(p < LO, has[0], jnp.where(p > HI, has[1], True))
        return jnp.where(there, 1.0, 0.0)

    def forward(src_u, src_v, dst_u, dst_v, halo):
        def body(p, r, n):
            u, lap_u = lap(src_u, p, r, n)
            v, lap_v = lap(src_v, p, r, n)
            rate = held(F, p, r, n)
            react = u * v * v
            supply = 0.1 * LAB[pl.ds(r, n), :].astype(jnp.float32)
            new_u = u + diff_u * lap_u - react + rate * (1.0 - u) + supply
            new_v = v + diff_v * lap_v + react - (rate + kill) * v
            if halo:
                keep = halo_mask(p)
                new_u, new_v = new_u * keep, new_v * keep
            dst_u[p, pl.ds(r, n), :] = new_u
            dst_v[p, pl.ds(r, n), :] = new_v

        return body

    def first_tangent(p, r, n):
        shift = held(D, p, r, n)
        P1[p, pl.ds(r, n), :] = (1.0 - held(U0, p, r, n)) * shift
        Q1[p, pl.ds(r, n), :] = -held(V0, p, r, n) * shift

    def tangent(src_p, src_q, dst_p, dst_q, at_u, at_v, halo):
        def body(p, r, n):
            tan_p, lap_p = lap(src_p, p, r, n)
            tan_q, lap_q = lap(src_q, p, r, n)
            u, v = held(at_u, p, r, n), held(at_v, p, r, n)
            rate, shift = held(F, p, r, n), held(D, p, r, n)
            sq = v * v
            both = 2.0 * (u * v)
            new_p = tan_p + diff_u * lap_p - (sq + rate) * tan_p - both * tan_q + (1.0 - u) * shift
            new_q = tan_q + diff_v * lap_q + sq * tan_p + (both - rate - kill) * tan_q - v * shift
            if halo:
                keep = halo_mask(p)
                new_p, new_q = new_p * keep, new_q * keep
            dst_p[p, pl.ds(r, n), :] = new_p
            dst_q[p, pl.ds(r, n), :] = new_q

        return body

    def adjoint(src_a, src_b, at_u, at_v, p, r, n):
        a, lap_a = lap(src_a, p, r, n)
        b, lap_b = lap(src_b, p, r, n)
        u, v = held(at_u, p, r, n), held(at_v, p, r, n)
        rate = held(F, p, r, n)
        sq = v * v
        both = 2.0 * (u * v)
        new_a = a + diff_u * lap_a - (sq + rate) * a + sq * b
        new_b = b + diff_v * lap_b - both * a + (both - rate - kill) * b
        return a, b, u, v, new_a, new_b

    def second_adjoint(p, r, n):
        new_a, new_b = adjoint(A3, B3, U2, V2, p, r, n)[4:]
        A2[p, pl.ds(r, n), :] = new_a
        B2[p, pl.ds(r, n), :] = new_b

    def product(p, r, n):
        a, b, u, v, new_a, new_b = adjoint(A2, B2, U1, V1, p, r, n)
        total = (1.0 - held(U2, p, r, n)) * held(A3, p, r, n) - held(V2, p, r, n) * held(B3, p, r, n)
        total = total + (1.0 - u) * a - v * b
        total = total + (1.0 - held(U0, p, r, n)) * new_a - held(V0, p, r, n) * new_b
        G[p - LO, pl.ds(row(r - start), n), :] = total

    inner, ends, halos = (3, 1, 2), (2, 3, 2), (1, 5, 2)
    for copy in loads:
        copy.wait()
    for arrived in got_mate:
        arrived()
    sweep(inner, forward(U0, V0, U1, V1, False))

    for arrived in got_dir + got_feed:
        arrived()
    passed = []
    for side in (0, 1):
        planes = ((0, 2), (6, 8))[side]
        for step in range(1, exps):
            for ref in (
                D.at[planes[0] : planes[1], pl.ds(mine, part)],
                F.at[(1, 6)[side], pl.ds(mine, part)],
            ):
                passed.append(remote(ref, ref, peer(step=step), has[side], has[side]))
    for arrived in got_rows + passed:
        arrived()
    mate_row = row(start + edge_in)
    got_edges = [remote(
        D.at[:, pl.ds(mate_row, EDGE)], D.at[:, pl.ds(edge_out, EDGE)], peer(other=True))]
    for p in (1, 6):
        got_edges.append(remote(
            F.at[p, pl.ds(mate_row, EDGE)], F.at[p, pl.ds(edge_out, EDGE)], peer(other=True)))

    for arrived in got_one:
        arrived()
    sweep(ends, forward(U0, V0, U1, V1, False))
    sweep(inner, forward(U1, V1, U2, V2, False))
    for arrived in got_edges:
        arrived()
    sweep((1, 1, 6), first_tangent)
    sweep((2, 1, 4), tangent(P1, Q1, P2, Q2, U1, V1, False))
    sweep(inner, tangent(P2, Q2, A3, B3, U2, V2, False))

    for arrived in got_two:
        arrived()
    sweep((0, 7, 2), first_tangent)
    sweep(halos, forward(U0, V0, U1, V1, True))
    sweep(halos, tangent(P1, Q1, P2, Q2, U1, V1, True))
    sweep(ends, forward(U1, V1, U2, V2, False))
    sweep(ends, tangent(P2, Q2, A3, B3, U2, V2, False))
    got_adj = []
    for side in (0, 1):
        for ref in (A3, B3):
            got_adj.append(remote(
                ref.at[(LO, HI)[side], pl.ds(PAD, rows)],
                ref.at[first_in[side], pl.ds(PAD, rows)],
                peer(side), has[side], has[1 - side]))
    sweep(inner, second_adjoint)
    for arrived in got_adj:
        arrived()
    sweep(ends, second_adjoint)

    got_add = []
    for side in (0, 1):
        p, q = (LO, HI)[side], (1, 6)[side]

        def block(j, carry):
            r = row(start + j * CHUNK)
            C[side, pl.ds(row(j * CHUNK), CHUNK), :] = (
                (1.0 - held(U0, q, r, CHUNK)) * (diff_u * held(A2, p, r, CHUNK))
                - held(V0, q, r, CHUNK) * (diff_v * held(B2, p, r, CHUNK))
            )
            return carry

        lax.fori_loop(0, own // CHUNK, block, 0)
        got_add.append(remote(C.at[side], CN.at[1 - side], peer(side), has[side], has[1 - side]))

    def scatter(which):
        sent = []
        for step in range(1, exps):
            theirs = row(part * lax.rem(exp + step, exps))
            for p in which:
                sent.append(remote(
                    G.at[p, pl.ds(theirs, part)], R.at[step - 1, p], peer(step=step)))
        return sent

    sweep(inner, product, start, own)
    got_sum = scatter((1, 2))
    sweep(ends, product, start, own)
    for arrived in got_add:
        arrived()
    for side in (0, 1):
        def block(j, carry):
            r = pl.ds(row(j * CHUNK), CHUNK)
            G[(0, 3)[side], r, :] += CN[side, r, :]
            return carry

        lax.fori_loop(0, own // CHUNK, block, 0)
    got_sum += scatter((0, 3))
    for arrived in got_sum:
        arrived()
    kept = row(part * exp)
    for p in range(4):
        total = G[p, pl.ds(kept, part), :]
        for step in range(1, exps):
            total = total + R[step - 1, p]
        out[p] = total
    for sends, copy in pending:
        if sends is None:
            copy.wait_send()
        else:
            pl.when(sends)(copy.wait_send)


def solution(mesh):
    slabs, exps = mesh.shape["slab"], mesh.shape["exp"]

    def per_device(start_u, start_v, feed, labels, direction):
        planes, own, width = feed.shape
        part = own // exps
        tall = own + EDGE + 2 * PAD

        def field(*shape):
            return pltpu.VMEM(shape, jnp.float32)

        copies = 64 + 20 * exps
        return pl.pallas_call(
            functools.partial(kernel, slabs, exps),
            out_shape=jax.ShapeDtypeStruct((planes, part, width), jnp.float32),
            in_specs=[pl.BlockSpec(memory_space=pl.ANY)] * 5,
            out_specs=pl.BlockSpec(memory_space=pltpu.VMEM),
            scratch_shapes=(
                [field(8, tall, width)] * 4
                + [pltpu.VMEM((tall, width), jnp.int32)]
                + [field(8, tall, width)] * 12
                + [
                    field(2, own, width),
                    field(2, own, width),
                    field(planes, own, width),
                    field(exps - 1, planes, part, width),
                    pltpu.SemaphoreType.DMA((copies,)),
                    pltpu.SemaphoreType.DMA((copies,)),
                    pltpu.SemaphoreType.DMA((5,)),
                ]
            ),
            compiler_params=pltpu.CompilerParams(
                collective_id=0, has_side_effects=True, vmem_limit_bytes=48 * 1024 * 1024
            ),
        )(start_u[0], start_v[0], feed, labels[0], direction)

    placed = (
        P(("grp", "exp"), "slab", "sub", None),
        P(("grp", "exp"), "slab", "sub", None),
        P(("grp", "slab"), "sub", None),
        P(("grp", "exp"), "sub", None),
        P(("grp", "slab"), ("sub", "exp"), None),
    )
    return jax.shard_map(
        per_device,
        mesh=mesh,
        in_specs=placed,
        out_specs=P(("grp", "slab"), ("sub", "exp"), None),
        check_vma=False,
    )
```

time: 133 us -> 54.9 us (0.41)
  starting transfers between devices: 56.8 us -> 0 us
  Pallas kernels: 0 us -> 48.9 us
  waiting for transfers between devices: 41.9 us -> 0 us
  between operations: 13.8 us -> 0.01 us
  other arithmetic: 10.4 us -> 0 us
  blocking collectives: 8.44 us -> 0 us
  local copies, waits for them, and re-layouts: 0.55 us -> 5.68 us
    ppermute x24 -> x0, starting transfers between devices: 56.8 us -> none  [the longest x12 41.3 us: extended(): lax.ppermute(tail, axis, [(i, (i + 1) % count) for i in range(ends)])]
    pallas_call x0 -> x1, Pallas kernels: none -> 48.9 us  [per_device(): pl.pallas_call(functools.partial(kernel, slabs, exps), out_shape=jax.Shap...]
    ppermute x24 -> x0, waiting for transfers between devices: 28.9 us -> none  [the longest x12 16 us: extended(): lax.ppermute(head, axis, [((i + 1) % count, i) for i in range(ends)])]
    reduce_scatter x1 -> x0, waiting for transfers between devices: 12.9 us -> none  [per_device(): return lax.psum_scatter(partial_sum, 'exp', scatter_dimension=1, tiled=True)]
    all_gather x1 -> x0, blocking collectives: 8.44 us -> none  [per_device(): shift = lax.all_gather(direction, 'exp', axis=1, tiled=True)]
    unnamed x10 -> x11, local copies, waits for them, and re-layouts: 0.55 us -> 5.68 us
    another operation x14 -> x0, other arithmetic: 3.94 us -> none  [the longest x2 1.56 us: per_device(): anchor = jnp.stack([start_u, start_v], 1)]
    sub x8 -> x0, other arithmetic: 3.62 us -> none  [the longest x6 3.06 us: laplace(): return total - 6.0 * core]
  transfers between devices with their start and end apart: 25 -> 0, of which waited for: 13 -> 0; matrix products, arithmetic and copies ran while one was open for 3% -> 0% of each run, Pallas kernels for 0% -> 0%
where the time goes in v1:
time: 54.9 us; the launch traced here: 54.6 us
  Pallas kernels  48.9 us (89%)
  local copies, waits for them, and re-layouts  5.68 us (10%)
    pallas_call x1, Pallas kernels, per_device(): pl.pallas_call(functools.partial(kernel, slabs, exps), out_shape=jax.Shap...  48.9 us
    unnamed x11, local copies, waits for them, and re-layouts  5.68 us

profile of v1, /device:TPU:0, one launch (start us, length us, event | category | flops | bytes accessed | tf_op | source)
XLA Modules:
  0.0 54.6 jit_solution(4172886720155641599)
XLA Ops:
  0.0 0.0 copy-start
  0.0 1.0 %copy-done = f32[1,4,128,256]{3,2,1,0:T(8,128)S(1)} copy-done((f32[1,4,128,256]{3,2,1,0:T(8,128)S(1)}, f32[1,4,128,256]{3,2,1,0:T(8,128)}, u32[]{:S(2)}) %copy-start) | copy-done | bytes 524312
  1.0 0.0 copy-start.1
  1.0 1.0 %copy-done.1 = f32[1,4,128,256]{3,2,1,0:T(8,128)S(1)} copy-done((f32[1,4,128,256]{3,2,1,0:T(8,128)S(1)}, f32[1,4,128,256]{3,2,1,0:T(8,128)}, u32[]{:S(2)}) %copy-start.1) | copy-done | bytes 524312
  2.1 0.0 copy-start.2
  2.1 1.0 %copy-done.2 = f32[4,128,256]{2,1,0:T(8,128)S(1)} copy-done((f32[4,128,256]{2,1,0:T(8,128)S(1)}, f32[4,128,256]{2,1,0:T(8,128)}, u32[]{:S(2)}) %copy-start.2) | copy-done | bytes 524312
  3.1 0.0 copy-start.3
  3.1 0.9 %copy-done.3 = f32[4,64,256]{2,1,0:T(8,128)S(1)} copy-done((f32[4,64,256]{2,1,0:T(8,128)S(1)}, f32[4,64,256]{2,1,0:T(8,128)}, u32[]{:S(2)}) %copy-start.3) | copy-done | bytes 262168
  4.1 0.0 copy-start.4
  4.1 0.9 %copy-done.4 = s32[1,128,256]{2,1,0:T(8,128)S(1)} copy-done((s32[1,128,256]{2,1,0:T(8,128)S(1)}, s32[1,128,256]{2,1,0:T(8,128)}, u32[]{:S(2)}) %copy-start.4) | copy-done | bytes 131096
  5.0 48.9 %shard_map.55 = f32[4,64,256]{2,1,0:T(8,128)S(1)} custom-call(f32[4,128,256]{2,1,0:T(8,128)S(1)} %bitcast.3, f32[4,128,256]{2,1,0:T(8,128)S(1)} %bitcast.4, f32[4,128,256]{2,1,0:T(8,128)S(1)} %copy-done.2, s32[128,256]{1,0:T(8,128)S(1)} %bitcast.5, f32[4,64,256]{2,1,0:T(8,128)S(1)} %copy-done.3), custom_call_target="tpu_custom_call" | custom-call | tf_op jit(solution)/shard_map/pallas_call | solution.py:379
  53.9 0.7 %copy.7 = f32[4,64,256]{2,1,0:T(8,128)} copy(f32[4,64,256]{2,1,0:T(8,128)S(1)} %shard_map.55) | data formatting | bytes 524288
Async XLA Ops:
  0.0 1.0 %copy-start = (f32[1,4,128,256]{3,2,1,0:T(8,128)S(1)}, f32[1,4,128,256]{3,2,1,0:T(8,128)}, u32[]{:S(2)}) copy-start(f32[1,4,128,256]{3,2,1,0:T(8,128)} %param.5) | copy-start | bytes 1572868
  1.0 1.0 %copy-start.1 = (f32[1,4,128,256]{3,2,1,0:T(8,128)S(1)}, f32[1,4,128,256]{3,2,1,0:T(8,128)}, u32[]{:S(2)}) copy-start(f32[1,4,128,256]{3,2,1,0:T(8,128)} %param.6) | copy-start | bytes 1572868
  2.1 1.0 %copy-start.2 = (f32[4,128,256]{2,1,0:T(8,128)S(1)}, f32[4,128,256]{2,1,0:T(8,128)}, u32[]{:S(2)}) copy-start(f32[4,128,256]{2,1,0:T(8,128)} %feed_in.1) | copy-start | bytes 1572868
  3.1 0.9 %copy-start.3 = (f32[4,64,256]{2,1,0:T(8,128)S(1)}, f32[4,64,256]{2,1,0:T(8,128)}, u32[]{:S(2)}) copy-start(f32[4,64,256]{2,1,0:T(8,128)} %dir_in.1) | copy-start | bytes 786436
  4.1 0.9 %copy-start.4 = (s32[1,128,256]{2,1,0:T(8,128)S(1)}, s32[1,128,256]{2,1,0:T(8,128)}, u32[]{:S(2)}) copy-start(s32[1,128,256]{2,1,0:T(8,128)} %param.8) | copy-start | bytes 393220

commit v2 on v1

--- a/solution.py
+++ b/solution.py
@@ -153,11 +153,21 @@
             got_one.append(remote(
                 src.at[a:b, pl.ds(edge_in, EDGE)], dst.at[c:d, pl.ds(edge_out, EDGE)],
                 peer(side, other=True), has[side], has[1 - side]))
-    for side in (0, 1):
-        for src, dst in ((u_in, U0), (v_in, V0)):
-            got_two.append(remote(
-                src.at[second[side]], dst.at[second_in[side], pl.ds(start, own)],
-                peer(side), has[side], has[1 - side]))
+    upward = 2 * exp >= exps
+    blocks = own // CHUNK
+
+    def top(k):
+        return row(CHUNK * jnp.where(upward, k, blocks - 1 - k))
+
+    for k in range(blocks):
+        got = []
+        for side in (0, 1):
+            for src, dst in ((u_in, U0), (v_in, V0)):
+                got.append(remote(
+                    src.at[second[side], pl.ds(top(k), CHUNK)],
+                    dst.at[second_in[side], pl.ds(row(start + top(k)), CHUNK)],
+                    peer(side), has[side], has[1 - side]))
+        got_two.append(got)
 
     def sweep(planes, body, first=PAD, length=rows):
         begin, stride, number = planes
@@ -293,64 +303,82 @@
     sweep((2, 1, 4), tangent(P1, Q1, P2, Q2, U1, V1, False))
     sweep(inner, tangent(P2, Q2, A3, B3, U2, V2, False))
 
-    for arrived in got_two:
-        arrived()
-    sweep((0, 7, 2), first_tangent)
-    sweep(halos, forward(U0, V0, U1, V1, True))
-    sweep(halos, tangent(P1, Q1, P2, Q2, U1, V1, True))
-    sweep(ends, forward(U1, V1, U2, V2, False))
-    sweep(ends, tangent(P2, Q2, A3, B3, U2, V2, False))
+    pieces = [([], row(PAD + own * mate), EDGE)]
+    pieces += [(got_two[k], row(start + top(k)), CHUNK) for k in range(blocks)]
     got_adj = []
-    for side in (0, 1):
-        for ref in (A3, B3):
-            got_adj.append(remote(
-                ref.at[(LO, HI)[side], pl.ds(PAD, rows)],
-                ref.at[first_in[side], pl.ds(PAD, rows)],
+    for waits, first, length in pieces:
+        for arrived in waits:
+            arrived()
+        sweep((0, 7, 2), first_tangent, first, length)
+        sweep(halos, forward(U0, V0, U1, V1, True), first, length)
+        sweep(halos, tangent(P1, Q1, P2, Q2, U1, V1, True), first, length)
+        sweep(ends, forward(U1, V1, U2, V2, False), first, length)
+        sweep(ends, tangent(P2, Q2, A3, B3, U2, V2, False), first, length)
+        got = []
+        for side in (0, 1):
+            for ref in (A3, B3):
+                got.append(remote(
+                    ref.at[(LO, HI)[side], pl.ds(first, length)],
+                    ref.at[first_in[side], pl.ds(first, length)],
+                    peer(side), has[side], has[1 - side]))
+        got_adj.append(got)
+    sweep(inner, second_adjoint)
+
+    span = part // CHUNK
+    base = count[0]
+    count[0] += (exps - 1) * span
+    got_add, leaving = [], []
+
+    def finish(k):
+        at = top(k)
+        sweep((LO, 1, 4), product, row(start + at), CHUNK)
+        for arrived in got_add[k]:
+            arrived()
+        for side in (0, 1):
+            G[(0, 3)[side], pl.ds(at, CHUNK), :] += CN[side, pl.ds(at, CHUNK), :]
+        step = lax.rem(at // part + exps - exp, exps)
+        within = lax.rem(at, part)
+        away = step > 0
+        slot = jnp.maximum(step - 1, 0)
+        i = base + slot * span + within // CHUNK
+        copy = pltpu.make_async_remote_copy(
+            src_ref=G.at[:, pl.ds(at, CHUNK)],
+            dst_ref=R.at[slot, :, pl.ds(row(within), CHUNK)],
+            send_sem=send.at[i], recv_sem=recv.at[i],
+            device_id=peer(step=jnp.maximum(step, 1)), device_id_type=MESH,
+        )
+        pl.when(away)(copy.start)
+        pending.append((away, copy))
+
+    for k, (waits, first, length) in enumerate([(got_adj[0], *pieces[0][1:])] + [
+        (got_adj[k + 1], *pieces[k + 1][1:]) for k in range(blocks)
+    ]):
+        for arrived in waits:
+            arrived()
+        sweep(ends, second_adjoint, first, length)
+        if k == 0:
+            continue
+        at = top(k - 1)
+        got = []
+        for side in (0, 1):
+            p, q = (LO, HI)[side], (1, 6)[side]
+            C[side, pl.ds(at, CHUNK), :] = (
+                (1.0 - held(U0, q, first, CHUNK)) * (diff_u * held(A2, p, first, CHUNK))
+                - held(V0, q, first, CHUNK) * (diff_v * held(B2, p, first, CHUNK))
+            )
+            got.append(remote(
+                C.at[side, pl.ds(at, CHUNK)], CN.at[1 - side, pl.ds(at, CHUNK)],
                 peer(side), has[side], has[1 - side]))
-    sweep(inner, second_adjoint)
-    for arrived in got_adj:
-        arrived()
-    sweep(ends, second_adjoint)
-
-    got_add = []
-    for side in (0, 1):
-        p, q = (LO, HI)[side], (1, 6)[side]
-
-        def block(j, carry):
-            r = row(start + j * CHUNK)
-            C[side, pl.ds(row(j * CHUNK), CHUNK), :] = (
-                (1.0 - held(U0, q, r, CHUNK)) * (diff_u * held(A2, p, r, CHUNK))
-                - held(V0, q, r, CHUNK) * (diff_v * held(B2, p, r, CHUNK))
-            )
-            return carry
-
-        lax.fori_loop(0, own // CHUNK, block, 0)
-        got_add.append(remote(C.at[side], CN.at[1 - side], peer(side), has[side], has[1 - side]))
-
-    def scatter(which):
-        sent = []
-        for step in range(1, exps):
-            theirs = row(part * lax.rem(exp + step, exps))
-            for p in which:
-                sent.append(remote(
-                    G.at[p, pl.ds(theirs, part)], R.at[step - 1, p], peer(step=step)))
-        return sent
-
-    sweep(inner, product, start, own)
-    got_sum = scatter((1, 2))
-    sweep(ends, product, start, own)
-    for arrived in got_add:
-        arrived()
-    for side in (0, 1):
-        def block(j, carry):
-            r = pl.ds(row(j * CHUNK), CHUNK)
-            G[(0, 3)[side], r, :] += CN[side, r, :]
-            return carry
-
-        lax.fori_loop(0, own // CHUNK, block, 0)
-    got_sum += scatter((0, 3))
-    for arrived in got_sum:
-        arrived()
+        got_add.append(got)
+        if k > 1:
+            finish(k - 2)
+    finish(blocks - 1)
+
+    for step in range(1, exps):
+        for m in range(span):
+            rows_in = R.at[step - 1, :, pl.ds(m * CHUNK, CHUNK)]
+            i = base + (step - 1) * span + m
+            pltpu.make_async_copy(rows_in, rows_in, recv.at[i]).wait()
     kept = row(part * exp)
     for p in range(4):
         total = G[p, pl.ds(kept, part), :]
@@ -375,11 +403,11 @@
         def field(*shape):
             return pltpu.VMEM(shape, jnp.float32)
 
-        copies = 64 + 20 * exps
+        copies = 128 + 16 * exps
         return pl.pallas_call(
             functools.partial(kernel, slabs, exps),
             out_shape=jax.ShapeDtypeStruct((planes, part, width), jnp.float32),
-            in_specs=[pl.BlockSpec(memory_space=pl.ANY)] * 5,
+            in_specs=[pl.BlockSpec(memory_space=pltpu.HBM)] * 5,
             out_specs=pl.BlockSpec(memory_space=pltpu.VMEM),
             scratch_shapes=(
                 [field(8, tall, width)] * 4
@@ -396,7 +424,7 @@
                 ]
             ),
             compiler_params=pltpu.CompilerParams(
-                collective_id=0, has_side_effects=True, vmem_limit_bytes=48 * 1024 * 1024
+                collective_id=0, has_side_effects=True, vmem_limit_bytes=62 * 1024 * 1024
             ),
         )(start_u[0], start_v[0], feed, labels[0], direction)
 

time: 54.9 us -> 47.6 us (0.87)
  local copies, waits for them, and re-layouts: 5.68 us -> 1.67 us
  Pallas kernels: 48.9 us -> 45.8 us
    unnamed x11 -> x1, local copies, waits for them, and re-layouts: 5.68 us -> 1.67 us
    pallas_call x1, Pallas kernels: 48.9 us -> 45.8 us  [per_device(): pl.pallas_call(functools.partial(kernel, slabs, exps), out_shape=jax.Shap...]
where the time goes in v2:
time: 47.6 us; the launch traced here: 47.5 us
  Pallas kernels  45.8 us (96%)
  local copies, waits for them, and re-layouts  1.67 us (4%)
    pallas_call x1, Pallas kernels, per_device(): pl.pallas_call(functools.partial(kernel, slabs, exps), out_shape=jax.Shap...  45.8 us
    unnamed x1, local copies, waits for them, and re-layouts  1.67 us

profile of v2, /device:TPU:0, one launch (start us, length us, event | category | flops | bytes accessed | tf_op | source)
XLA Modules:
  0.0 47.5 jit_solution(2116069074383638823)
XLA Ops:
  0.0 45.8 %shard_map.55 = f32[4,64,256]{2,1,0:T(8,128)} custom-call(f32[4,128,256]{2,1,0:T(8,128)} %bitcast.3, f32[4,128,256]{2,1,0:T(8,128)} %bitcast.4, f32[4,128,256]{2,1,0:T(8,128)} %feed_in.1, s32[128,256]{1,0:T(8,128)} %bitcast.5, f32[4,64,256]{2,1,0:T(8,128)} %dir_in.1), custom_call_target="tpu_custom_call" | custom-call | tf_op jit(solution)/shard_map/pallas_call | solution.py:407
  45.8 1.7 %copy.7 = f32[4,64,256]{2,1,0:T(8,128)} copy(f32[4,64,256]{2,1,0:T(8,128)} %shard_map.55) | data formatting | bytes 524288

commit v3 on v2

--- a/solution.py
+++ b/solution.py
@@ -14,6 +14,7 @@
 EDGE = 8
 PAD = 8
 CHUNK = 32
+BLOCK = 16
 LO, HI = 2, 5
 MESH = pl.DeviceIdType.MESH
 
@@ -176,15 +177,15 @@
             p = begin + stride * i
 
             def block(j, inner):
-                body(p, row(first + j * CHUNK), CHUNK)
+                body(p, row(first + j * BLOCK), BLOCK)
                 return inner
 
-            lax.fori_loop(0, length // CHUNK, block, 0)
-            if length % CHUNK:
-                body(p, row(first + length // CHUNK * CHUNK), length % CHUNK)
+            lax.fori_loop(0, length // BLOCK, block, 0, unroll=True)
+            if length % BLOCK:
+                body(p, row(first + length // BLOCK * BLOCK), length % BLOCK)
             return carry
 
-        lax.fori_loop(0, number, plane, 0)
+        lax.fori_loop(0, number, plane, 0, unroll=length <= CHUNK)
 
     def held(ref, p, r, n):
         return ref[p, pl.ds(r, n), :]

time: 47.6 us -> 45.4 us (0.954)
  Pallas kernels: 45.8 us -> 43.6 us
    pallas_call x1, Pallas kernels: 45.8 us -> 43.6 us  [per_device(): pl.pallas_call(functools.partial(kernel, slabs, exps), out_shape=jax.Shap...]
where the time goes in v3:
time: 45.4 us; the launch traced here: 45.3 us
  Pallas kernels  43.6 us (96%)
  local copies, waits for them, and re-layouts  1.67 us (4%)
    pallas_call x1, Pallas kernels, per_device(): pl.pallas_call(functools.partial(kernel, slabs, exps), out_shape=jax.Shap...  43.6 us
    unnamed x1, local copies, waits for them, and re-layouts  1.67 us

profile of v3, /device:TPU:0, one launch (start us, length us, event | category | flops | bytes accessed | tf_op | source)
XLA Modules:
  0.0 45.3 jit_solution(4351205247510629139)
XLA Ops:
  0.0 43.6 %shard_map.55 = f32[4,64,256]{2,1,0:T(8,128)} custom-call(f32[4,128,256]{2,1,0:T(8,128)} %bitcast.3, f32[4,128,256]{2,1,0:T(8,128)} %bitcast.4, f32[4,128,256]{2,1,0:T(8,128)} %feed_in.1, s32[128,256]{1,0:T(8,128)} %bitcast.5, f32[4,64,256]{2,1,0:T(8,128)} %dir_in.1), custom_call_target="tpu_custom_call" | custom-call | tf_op jit(solution)/shard_map/pallas_call | solution.py:408
  43.6 1.7 %copy.7 = f32[4,64,256]{2,1,0:T(8,128)} copy(f32[4,64,256]{2,1,0:T(8,128)} %shard_map.55) | data formatting | bytes 524288

commit v4 on v3

--- a/solution.py
+++ b/solution.py
@@ -22,11 +22,12 @@
 def kernel(
     slabs, exps,
     u_in, v_in, feed_in, lab_in, dir_in, out,
-    U0, V0, D, F, LAB, U1, V1, U2, V2, P1, Q1, P2, Q2, A3, B3, A2, B2,
+    U0, V0, D, F, LAB, U1, V1, U2, V2, P1, Q1, P2, Q2, AB, A2, B2,
     C, CN, G, R, send, recv, local,
 ):
     own, width = u_in.shape[1], u_in.shape[2]
     rows = own + EDGE
+    A3, B3 = AB.at[0], AB.at[1]
     part = own // exps
     grp, slab = lax.axis_index("grp"), lax.axis_index("slab")
     exp, sub = lax.axis_index("exp"), lax.axis_index("sub")
@@ -69,6 +70,20 @@
 
         return arrived
 
+    barrier = pltpu.get_barrier_semaphore()
+
+    def greet(target):
+        pl.semaphore_signal(barrier, inc=1, device_id=target, device_id_type=MESH)
+
+    greet(peer(other=True))
+    for step in range(1, exps):
+        greet(peer(step=step))
+    for side in (0, 1):
+        @pl.when(has[side])
+        def _():
+            greet(peer(side))
+            greet(peer(side, other=True))
+
     loads = []
     for i, (src, dst) in enumerate([
         (u_in, U0.at[LO : HI + 1, pl.ds(start, own)]),
@@ -80,20 +95,6 @@
         copy = pltpu.make_async_copy(src, dst, local.at[i])
         copy.start()
         loads.append(copy)
-
-    barrier = pltpu.get_barrier_semaphore()
-
-    def greet(target):
-        pl.semaphore_signal(barrier, inc=1, device_id=target, device_id_type=MESH)
-
-    greet(peer(other=True))
-    for step in range(1, exps):
-        greet(peer(step=step))
-    for side in (0, 1):
-        @pl.when(has[side])
-        def _():
-            greet(peer(side))
-            greet(peer(side, other=True))
 
     for ref in (U0, V0, U1, V1, P1, Q1, P2, Q2, A3, B3, A2, B2):
         blank = jnp.zeros((ref.shape[0], PAD, width), jnp.float32)
@@ -317,11 +318,10 @@
         sweep(ends, tangent(P2, Q2, A3, B3, U2, V2, False), first, length)
         got = []
         for side in (0, 1):
-            for ref in (A3, B3):
-                got.append(remote(
-                    ref.at[(LO, HI)[side], pl.ds(first, length)],
-                    ref.at[first_in[side], pl.ds(first, length)],
-                    peer(side), has[side], has[1 - side]))
+            got.append(remote(
+                AB.at[:, (LO, HI)[side], pl.ds(first, length)],
+                AB.at[:, first_in[side], pl.ds(first, length)],
+                peer(side), has[side], has[1 - side]))
         got_adj.append(got)
     sweep(inner, second_adjoint)
 
@@ -413,7 +413,9 @@
             scratch_shapes=(
                 [field(8, tall, width)] * 4
                 + [pltpu.VMEM((tall, width), jnp.int32)]
-                + [field(8, tall, width)] * 12
+                + [field(8, tall, width)] * 8
+                + [field(2, 8, tall, width)]
+                + [field(8, tall, width)] * 2
                 + [
                     field(2, own, width),
                     field(2, own, width),

time: 45.4 us -> 45.4 us (level)
  no operation moved by 1% of the time
where the time goes in v4:
time: 45.4 us; the launch traced here: 45.3 us
  Pallas kernels  43.6 us (96%)
  local copies, waits for them, and re-layouts  1.67 us (4%)
    pallas_call x1, Pallas kernels, per_device(): pl.pallas_call(functools.partial(kernel, slabs, exps), out_shape=jax.Shap...  43.6 us
    unnamed x1, local copies, waits for them, and re-layouts  1.67 us

profile of v4, /device:TPU:0, one launch (start us, length us, event | category | flops | bytes accessed | tf_op | source)
XLA Modules:
  0.0 45.3 jit_solution(2953141991847680195)
XLA Ops:
  0.0 43.6 %shard_map.55 = f32[4,64,256]{2,1,0:T(8,128)} custom-call(f32[4,128,256]{2,1,0:T(8,128)} %bitcast.3, f32[4,128,256]{2,1,0:T(8,128)} %bitcast.4, f32[4,128,256]{2,1,0:T(8,128)} %feed_in.1, s32[128,256]{1,0:T(8,128)} %bitcast.5, f32[4,64,256]{2,1,0:T(8,128)} %dir_in.1), custom_call_target="tpu_custom_call" | custom-call | tf_op jit(solution)/shard_map/pallas_call | solution.py:408
  43.6 1.7 %copy.7 = f32[4,64,256]{2,1,0:T(8,128)} copy(f32[4,64,256]{2,1,0:T(8,128)} %shard_map.55) | data formatting | bytes 524288
